TPU v7x, 32 devices: a whole 2x2x4 slice. The times are simulated.
32 devices in a mesh: grp: 2 (over y), own: 16 (over z, x, core).
Axes of the slice: x: 2, y: 2, z: 4, core: 2. Of those that a mesh axis runs over, the one named last changes fastest.
Arguments:
- amplitudes: bfloat16 [192, 32, 128], P('own', 'grp'), may hold values from -6 to 6
- integrals: bfloat16 [12288, 2048], P('own', 'grp'), may hold values from -0.109375 to 0.109375
- tile_block: int32 [192], P('own'), may hold values from 0 to 7, as said below
- tile_index: int32 [192], P('own'), may hold values from 0 to 95, as said below
Outputs:
- ladder: float32 [256, 2048], P('own', 'grp')
Inputs may be any that keep to these rules, and one draw needn't show every extreme that they name: Each pair (tile_block, tile_index) is named by at most one of the 192 tile rows. Of the 12 rows of one own index, at most 2 have tile_index in one owner's range o * 6 to (o + 1) * 6 - 1, and exactly 2 do for some owners. Exactly 12 of all tile rows have tile_index in each owner's range. `tile_index`: owner o holds integral rows of tiles o * 6 to (o + 1) * 6 - 1.
All inputs are finite; a program needn't handle non-finite values.
Results may differ from a plain program's by a relative error of at most 0.0003.
Values may be sent and summed in bfloat16 or wider, within the bound.
A program may use at most 64 MiB of HBM per device.

v0:
```python
import jax
import jax.numpy as jnp
from jax import lax
from jax.sharding import PartitionSpec as P

NB = 8
CAP = 2


def local(amplitudes, integrals, tile_block, tile_index):
    own_count = lax.axis_size("own")
    tile_width = amplitudes.shape[2]
    tile_dev = integrals.shape[0] // tile_width
    tile_owner = tile_index // tile_dev
    local_tile = tile_index - tile_owner * tile_dev
    tile_key = tile_block * tile_dev + local_tile
    one_hot = (tile_owner[:, None] == jnp.arange(own_count)[None, :]).astype(jnp.int32)
    slot_rank = jnp.sum((jnp.cumsum(one_hot, axis=0) - one_hot) * one_hot, axis=1)
    key_buffer = jnp.full((own_count, CAP), -1, jnp.int32).at[tile_owner, slot_rank].set(tile_key)
    gathered = lax.all_gather(amplitudes, "grp", axis=1, tiled=True)
    buffer = jnp.zeros((own_count, CAP) + gathered.shape[1:], gathered.dtype)
    received = lax.all_to_all(
        buffer.at[tile_owner, slot_rank].set(gathered),
        "own",
        split_axis=0,
        concat_axis=0,
        tiled=True,
    )
    recv_keys = lax.all_to_all(key_buffer, "own", split_axis=0, concat_axis=0, tiled=True)
    occ_rows = received.shape[2]
    slots = received.reshape(own_count * CAP, occ_rows, tile_width)
    flat_keys = recv_keys.reshape(own_count * CAP)
    recv_block = jnp.where(flat_keys >= 0, flat_keys // tile_dev, -1)
    recv_tile = jnp.where(flat_keys >= 0, flat_keys % tile_dev, 0)
    total_rows = NB * occ_rows
    row_count = total_rows // own_count * lax.axis_size("own")
    first_row = recv_block * occ_rows - jnp.int32(0)
    row_index = first_row[:, None] + jnp.arange(occ_rows)[None, :]
    in_range = (recv_block[:, None] >= 0) & (row_index >= 0) & (row_index < row_count)
    row_index = jnp.where(in_range, row_index, row_count)
    tile_slot = jnp.broadcast_to(recv_tile[:, None], row_index.shape)
    placed = jnp.zeros((row_count, tile_dev, tile_width), slots.dtype)
    placed = placed.at[row_index, tile_slot].set(slots, mode="drop")
    return lax.psum_scatter(
        jnp.dot(
            placed.reshape(row_count, tile_dev * tile_width),
            integrals,
            preferred_element_type=jnp.float32,
        ),
        "own",
        scatter_dimension=0,
        tiled=True,
    )


def solution(mesh):
    return jax.shard_map(
        local,
        mesh=mesh,
        in_specs=(P("own", "grp", None), P("own", "grp"), P("own"), P("own")),
        out_specs=P("own", "grp"),
        check_vma=False,
    )
```

profile of v0, /device:TPU:0, one launch (start us, length us, event | category | flops | bytes accessed | tf_op | source)
XLA Modules:
  0.0 108.6 jit_solution(2527903236008995986)
XLA Ops:
  6.5 0.0 copy-start
  6.5 0.0 copy-start.2
  6.5 0.0 copy-start.1
  6.5 0.8 subtract_add_fusion
  7.3 0.1 fusion.6
  7.5 0.2 select_reduce_fusion
  7.7 1.1 %scatter_fusion = s32[16,2]{0,1:T(2,128)S(1)} fusion(s32[16,2]{0,1:T(2,128)S(1)} %broadcast_in_dim.20, s32[12]{0:T(128)S(1)} %fusion.11, s32[12]{0:T(128)S(1)} %get-tuple-element.13), kind=kCustom, calls=%fused_computation | custom fusion | bytes 240 | tf_op jit(solution)/shard_map/scatter | solution.py:19
  8.8 0.7 copy.20
  9.5 7.4 %all-to-all-start = ((s32[16,1,2]{2,1,0:T(1,128)}), s32[16,1,2]{2,1,0:T(1,128)S(1)}, u32[]{:S(2)}, u32[]{:S(2)}) async-start(s32[16,1,2]{2,1,0:T(1,128)} %copy.20), calls=%async_computation | async-start | bytes 16384 | tf_op jit(solution)/shard_map/all_to_all | solution.py:29
  16.8 5.0 %all_gather.3 = bf16[12,32,128]{2,1,0:T(8,128)(2,1)S(1)} all-gather(bf16[12,16,128]{2,1,0:T(8,128)(2,1)} %param.4), channel_id=1, replica_groups=mesh['grp'=2,'own'=16] {'grp'}, dimensions={1}, use_global_device_ids=true | all-gather | bytes 147456 | tf_op jit(solution)/shard_map/all_gather | solution.py:20
  21.8 0.7 broadcast_in_dim.43
  22.6 2.2 %scatter_fusion.1 = bf16[16,2,32,128]{3,2,1,0:T(8,128)(2,1)} fusion(bf16[16,2,32,128]{3,2,1,0:T(8,128)(2,1)} %broadcast_in_dim.43, s32[12]{0:T(128)S(1)} %fusion.11, bf16[12,32,128]{2,1,0:T(8,128)(2,1)S(1)} %all_gather.3), kind=kCustom, calls=%fused_computation.1 | custom fusion | bytes 295008 | tf_op jit(solution)/shard_map/scatter | solution.py:23
  24.7 0.0 all-to-all-done
  24.7 6.0 %all-to-all-start.1 = ((bf16[16,2,32,128]{3,2,1,0:T(8,128)(2,1)}), bf16[16,2,32,128]{3,2,1,0:T(8,128)(2,1)S(1)}, u32[]{:S(2)}, u32[]{:S(2)}) async-start(bf16[16,2,32,128]{3,2,1,0:T(8,128)(2,1)} %scatter_fusion.1), calls=%async_computation.1 | async-start | bytes 524288 | tf_op jit(solution)/shard_map/all_to_all | solution.py:22
  30.7 0.0 reduce-scatter.2.cloned.1.call-start
  30.8 0.1 compare_reduce_fusion
  30.9 0.1 ne.61
  31.0 0.1 ge.37
  31.1 0.1 divide_reduce_fusion
  31.1 0.1 div.24
  31.2 0.1 rem.39
  31.4 0.1 compare_select_fusion
  31.4 0.0 copy-done.2
  31.5 0.1 multiply_reduce_fusion
  31.5 0.0 copy-done.1
  31.5 0.1 and_reduce_fusion
  31.6 0.1 reshape.237
  31.7 9.1 %all-to-all-done.1 = bf16[16,2,32,128]{3,2,1,0:T(8,128)(2,1)S(1)} async-done(((bf16[16,2,32,128]{3,2,1,0:T(8,128)(2,1)}), bf16[16,2,32,128]{3,2,1,0:T(8,128)(2,1)S(1)}, u32[]{:S(2)}, u32[]{:S(2)}) %all-to-all-start.1) | async-done | bytes 262176 | tf_op jit(solution)/shard_map/all_to_all | solution.py:22
  40.8 3.3 %scatter_custom_fusion.2 = bf16[1536,128]{1,0:T(8,128)(2,1)S(1)} fusion(s32[1024]{0:T(1024)S(1)} %reshape.237, bf16[1024,128]{1,0:T(8,128)(2,1)S(1)} %bitcast.26, bf16[]{:T(256)} %constant.16.clone.1), kind=kCustom, calls=%fused_computation.3 | custom fusion | bytes 393218
  44.1 0.2 copy.21
  44.3 0.0 copy-done
  44.3 1.6 %fusion.14 = f32[256,1024]{1,0:T(8,128)} fusion(bf16[256,768]{0,1:T(8,128)(2,1)S(1)} %bitcast.25, bf16[768,1024]{1,0:T(8,128)(2,1)S(1)} %copy-done), kind=kOutput, calls=%fused_computation.41 | convolution fusion | flops 402653184 | bytes 3014656 | tf_op jit(solution)/shard_map/dot_general | solution.py:45
  45.9 0.0 reduce-scatter.2.cloned.1.call-update
  45.9 55.8 %reduce-scatter.2.cloned.1.call-done = f32[16,1024]{1,0:T(8,128)} async-done(((f32[256,1024]{1,0:T(8,128)}), f32[16,1024]{1,0:T(8,128)}) %reduce-scatter.2.cloned.1.call-update) | async-done | bytes 65552 | tf_op jit(solution)/shard_map/reduce_scatter | solution.py:44
  (7 shorter events, 0.1 us)
Async XLA Ops:
  6.5 37.7 %copy-start = (bf16[768,1024]{1,0:T(8,128)(2,1)S(1)}, bf16[768,1024]{1,0:T(8,128)(2,1)}, u32[]{:S(2)}) copy-start(bf16[768,1024]{1,0:T(8,128)(2,1)} %param.5) | copy-start | bytes 4718596
  6.5 24.9 %copy-start.2 = (s32[2]{0:T(128)S(1)}, s32[2]{0:T(128)}, u32[]{:S(2)}) copy-start(s32[2]{0:T(128)} %constant.53) | copy-start | bytes 28
  6.5 25.0 %copy-start.1 = (s32[2]{0:T(128)S(1)}, s32[2]{0:T(128)}, u32[]{:S(2)}) copy-start(s32[2]{0:T(128)} %constant.56) | copy-start | bytes 28
  9.5 15.3 %all-to-all-start = ((s32[16,1,2]{2,1,0:T(1,128)}), s32[16,1,2]{2,1,0:T(1,128)S(1)}, u32[]{:S(2)}, u32[]{:S(2)}) async-start(s32[16,1,2]{2,1,0:T(1,128)} %copy.20), calls=%async_computation | async-start | bytes 16384 | tf_op jit(solution)/shard_map/all_to_all | solution.py:29
  24.7 16.1 %all-to-all-start.1 = ((bf16[16,2,32,128]{3,2,1,0:T(8,128)(2,1)}), bf16[16,2,32,128]{3,2,1,0:T(8,128)(2,1)S(1)}, u32[]{:S(2)}, u32[]{:S(2)}) async-start(bf16[16,2,32,128]{3,2,1,0:T(8,128)(2,1)} %scatter_fusion.1), calls=%async_computation.1 | async-start | bytes 524288 | tf_op jit(solution)/shard_map/all_to_all | solution.py:22
  30.7 71.0 %reduce-scatter.2.cloned.1.call-start = ((), (), s32[]{:S(2)}) async-start(), calls=%async_computation.3 | async-start | bytes 1114112 | tf_op jit(solution)/shard_map/reduce_scatter | solution.py:44
Sparse Core Ops, SparseCore 0:
  46.0 55.6 reduce-scatter.1
where the time goes:
time: 109 us
  waiting for transfers between devices  64.9 us (60%)
  between operations  13.5 us (12%)
  starting transfers between devices  13.4 us (12%)
  local copies, waits for them, and re-layouts  8.61 us (8%)
  blocking collectives  5 us (5%)
  matrix products  1.59 us (1%)
  other arithmetic  1.51 us (1%)
    reduce_scatter x1, waiting for transfers between devices, local(): lax.psum_scatter(jnp.dot(placed.reshape(row_count, tile_dev * tile_width)...  55.8 us
    all_to_all x1, waiting for transfers between devices, local(): lax.all_to_all(buffer.at[tile_owner, slot_rank].set(gathered), 'own', spl...  9.09 us
    all_to_all x1, starting transfers between devices, local(): lax.all_to_all(key_buffer, 'own', split_axis=0, concat_axis=0, tiled=True)  7.36 us
    all_to_all x1, starting transfers between devices, local(): lax.all_to_all(buffer.at[tile_owner, slot_rank].set(gathered), 'own', spl...  6 us
    all_gather x1, blocking collectives, local(): gathered = lax.all_gather(amplitudes, 'grp', axis=1, tiled=True)  5 us
    unnamed x8, local copies, waits for them, and re-layouts  3.37 us
  transfers between devices with their start and end apart: 3, of which 2 were waited for; matrix products, arithmetic and copies ran while one was open for 3% of the time, Pallas kernels for 0%

commit v1 on v0

--- a/solution.py
+++ b/solution.py
@@ -1,10 +1,17 @@
+import functools
+
 import jax
 import jax.numpy as jnp
 from jax import lax
+from jax.experimental import pallas as pl
+from jax.experimental.pallas import tpu as pltpu
 from jax.sharding import PartitionSpec as P
 
 NB = 8
 CAP = 2
+MESH = pl.DeviceIdType.MESH
+ORDER = (8, 7, 9, 6, 10, 5, 11, 4, 12, 3, 13, 2, 14, 1, 15)
+ZORDER = (2, 1, 3, 0)
 
 
 def local(amplitudes, integrals, tile_block, tile_index):
@@ -32,10 +39,8 @@
     flat_keys = recv_keys.reshape(own_count * CAP)
     recv_block = jnp.where(flat_keys >= 0, flat_keys // tile_dev, -1)
     recv_tile = jnp.where(flat_keys >= 0, flat_keys % tile_dev, 0)
-    total_rows = NB * occ_rows
-    row_count = total_rows // own_count * lax.axis_size("own")
-    first_row = recv_block * occ_rows - jnp.int32(0)
-    row_index = first_row[:, None] + jnp.arange(occ_rows)[None, :]
+    row_count = NB * occ_rows
+    row_index = recv_block[:, None] * occ_rows + jnp.arange(occ_rows)[None, :]
     in_range = (recv_block[:, None] >= 0) & (row_index >= 0) & (row_index < row_count)
     row_index = jnp.where(in_range, row_index, row_count)
     tile_slot = jnp.broadcast_to(recv_tile[:, None], row_index.shape)
@@ -53,11 +58,267 @@
     )
 
 
+def encode(v):
+    parts = [v[:, k * 128 : (k + 1) * 128] for k in range(8)]
+    top = functools.reduce(jnp.maximum, [jnp.abs(p) for p in parts])
+    expo = jnp.ceil(jnp.log2(jnp.maximum(top, 1e-30)))
+    scale = jnp.exp2(15.0 - expo)
+    coded = [jnp.clip(jnp.round(p * scale), -32767.0, 32767.0) for p in parts] + [expo]
+    return jnp.concatenate(coded, axis=1).astype(jnp.int32).astype(jnp.int16)
+
+
+def decode(q):
+    wide = q.astype(jnp.int32).astype(jnp.float32)
+    scale = jnp.exp2(wide[:, 1024:] - 15.0)
+    return jnp.concatenate([wide[:, k * 128 : (k + 1) * 128] * scale for k in range(8)], axis=1)
+
+
+def kernel(
+    block_ref, index_ref, amp_ref, int_hbm, out_ref,
+    ints, sends, recvs, others, key_out, key_in, pick, lhs, prod, sib,
+    x_out, x_in, z_out, z_in,
+    int_sem, tile_ss, tile_rs, key_ss, key_rs, fwd_ss, fwd_rs,
+    core_ss, core_rs, x_ss, x_rs, z_ss, z_rs,
+):
+    n = 16
+    rows = amp_ref.shape[0] // 16
+    tile_dev = 6
+    me = lax.axis_index("own")
+    g = lax.axis_index("grp")
+    core = lax.rem(me, 2)
+    x = lax.rem(me // 2, 2)
+    z = me // 4
+    sibling = me + 1 - 2 * core
+    across = me + 2 - 4 * x
+
+    load = pltpu.make_async_copy(int_hbm, ints, int_sem)
+    load.start()
+    barrier = pltpu.get_barrier_semaphore()
+    for d in range(1, n):
+        pl.semaphore_signal(barrier, inc=1, device_id={"own": lax.rem(me + d, n)}, device_id_type=MESH)
+    pl.semaphore_signal(barrier, inc=1, device_id={"grp": 1 - g}, device_id_type=MESH)
+
+    owner, rank, key = [], [], []
+    for r in range(rows):
+        t = index_ref[r]
+        o = t // tile_dev
+        owner.append(o)
+        key.append((t - o * tile_dev) * NB + block_ref[r])
+        earlier = jnp.int32(0)
+        for q in range(r):
+            earlier = earlier + jnp.where(owner[q] == o, 1, 0)
+        rank.append(earlier)
+
+    dest = lax.broadcasted_iota(jnp.int32, (n, 128), 0)
+    lane = lax.broadcasted_iota(jnp.int32, (n, 128), 1)
+    sub = lane - lax.rem(me, 4) * 32
+    slot = jnp.where((sub >= 0) & (sub < 32), dest * 2 + sub // 16, -1)
+    inner = lax.rem(lane, 16)
+    keys = jnp.zeros((n, 128), jnp.int32)
+    for r in range(rows):
+        keys = keys + jnp.where(slot == owner[r] * 2 + rank[r], key[r] * 16 + inner + 1, 0)
+    for o in range(n):
+        key_out[o] = keys[o : o + 1, :]
+
+    col = lax.broadcasted_iota(jnp.int32, (1, rows * 16), 1)
+    place = jnp.zeros((1, rows * 16), jnp.int32)
+    for r in range(rows):
+        place = jnp.where(col // 16 == r, (owner[r] * 2 + rank[r]) * 16 + lax.rem(col, 16), place)
+    amp = amp_ref[...]
+    for part in range(4):
+        row = lax.broadcasted_iota(jnp.int32, (128, rows * 16), 0) + part * 128
+        hot = jnp.where(row == place, 1.0, 0.0).astype(jnp.bfloat16)
+        got = jnp.dot(hot, amp, preferred_element_type=jnp.float32).astype(jnp.bfloat16)
+        sends[pl.ds(part * 4, 4)] = got.reshape(4, 32, 128)
+    recvs[me] = sends[me]
+    key_in[me] = key_out[me]
+
+    pl.semaphore_wait(barrier, n)
+
+    def key_copy(to):
+        return pltpu.make_async_remote_copy(
+            key_out.at[to], key_in.at[me], key_ss.at[to], key_rs.at[me],
+            device_id={"own": to}, device_id_type=MESH,
+        )
+
+    def tile_copy(to):
+        return pltpu.make_async_remote_copy(
+            sends.at[to], recvs.at[me], tile_ss.at[to], tile_rs.at[me],
+            device_id={"own": to}, device_id_type=MESH,
+        )
+
+    def forward(s):
+        return pltpu.make_async_remote_copy(
+            recvs.at[s], others.at[s], fwd_ss.at[s], fwd_rs.at[s],
+            device_id={"grp": 1 - g}, device_id_type=MESH,
+        )
+
+    for d in ORDER:
+        key_copy(lax.rem(me + d, n)).start()
+    for d in ORDER:
+        tile_copy(lax.rem(me + d, n)).start()
+    forward(me).start()
+
+    def arrived(s, buffer, sem):
+        return pltpu.make_async_remote_copy(
+            buffer.at[s], buffer.at[s], sem.at[s], sem.at[s],
+            device_id={"own": sibling}, device_id_type=MESH,
+        )
+
+    for d in ORDER:
+        arrived(lax.rem(me + n - d, n), key_in, key_rs).wait_recv()
+    targets = [
+        key_in[4 * j] + key_in[4 * j + 1] + key_in[4 * j + 2] + key_in[4 * j + 3] for j in range(4)
+    ]
+    target = jnp.concatenate(targets, axis=1)
+    for t in range(tile_dev):
+        row = lax.broadcasted_iota(jnp.int32, (128, 512), 0) + (t * 128 + 1)
+        pick[t] = jnp.where(row == target, 1.0, 0.0).astype(jnp.bfloat16)
+
+    for d in reversed(ORDER):
+        s = lax.rem(me + n - d, n)
+        arrived(s, recvs, tile_rs).wait_recv()
+        forward(s).start()
+
+    def half(h, source):
+        tiles = source[...].reshape(512, 128)
+        for t in range(tile_dev):
+            lhs[:, t * 128 : (t + 1) * 128] = jnp.dot(
+                pick[t], tiles, preferred_element_type=jnp.float32
+            ).astype(jnp.bfloat16)
+        if h == 0:
+            load.wait()
+        for k in range(4):
+            prod[h, k] = jnp.dot(
+                lhs[...], ints[:, k * 256 : (k + 1) * 256], preferred_element_type=jnp.float32
+            ).reshape(8, 16, 256)
+
+    def core_copy(h, k):
+        return pltpu.make_async_remote_copy(
+            prod.at[h, k], sib.at[k], core_ss.at[k], core_rs.at[k],
+            device_id={"own": sibling}, device_id_type=MESH,
+        )
+
+    mine_first = core == g
+
+    half(0, recvs)
+
+    @pl.when(jnp.logical_not(mine_first))
+    def _():
+        for k in range(4):
+            core_copy(0, k).start()
+
+    for d in range(n):
+        arrived(lax.rem(me + d, n), others, fwd_rs).wait_recv()
+    half(1, others)
+
+    @pl.when(mine_first)
+    def _():
+        for k in range(4):
+            core_copy(1, k).start()
+
+    for k in range(4):
+        core_copy(0, k).wait_recv()
+    keep = lax.rem(core + g, 2)
+
+    def chip_sum(b):
+        return jnp.concatenate([prod[keep, k, b] + sib[k, b] for k in range(4)], axis=1)
+
+    def x_copy(dz):
+        return pltpu.make_async_remote_copy(
+            x_out.at[dz], x_in.at[dz], x_ss.at[dz], x_rs.at[dz],
+            device_id={"own": across}, device_id_type=MESH,
+        )
+
+    def z_copy(dz):
+        return pltpu.make_async_remote_copy(
+            z_out.at[dz], z_in.at[dz], z_ss.at[dz], z_rs.at[dz],
+            device_id={"own": lax.rem(me + 4 * dz, n)}, device_id_type=MESH,
+        )
+
+    for dz in ZORDER:
+        to_z = lax.rem(z + dz, 4)
+        x_out[dz] = encode(chip_sum(to_z * 2 + 1 - x))
+        x_copy(dz).start()
+    for dz in ZORDER:
+        to_z = lax.rem(z + dz, 4)
+        total = chip_sum(to_z * 2 + x)
+        x_copy(dz).wait_recv()
+        total = total + decode(x_in[dz])
+        if dz:
+            z_out[dz] = encode(total)
+            z_copy(dz).start()
+        else:
+            out_ref[...] = total
+    for dz in (1, 3, 2):
+        z_copy(dz).wait_recv()
+        out_ref[...] += decode(z_in[dz])
+
+    for d in ORDER:
+        to = lax.rem(me + d, n)
+        key_copy(to).wait_send()
+        tile_copy(to).wait_send()
+    for s in range(n):
+        forward(s).wait_send()
+    for k in range(4):
+        core_copy(0, k).wait_send()
+    for dz in range(4):
+        x_copy(dz).wait_send()
+        if dz:
+            z_copy(dz).wait_send()
+
+
+def fused(amplitudes, integrals, tile_block, tile_index):
+    rows = amplitudes.shape[0]
+    dma = pltpu.SemaphoreType.DMA
+    bf16, f32, i32, i16 = jnp.bfloat16, jnp.float32, jnp.int32, jnp.int16
+    return pl.pallas_call(
+        kernel,
+        out_shape=jax.ShapeDtypeStruct((16, 1024), f32),
+        in_specs=[
+            pl.BlockSpec(memory_space=pltpu.SMEM),
+            pl.BlockSpec(memory_space=pltpu.SMEM),
+            pl.BlockSpec(memory_space=pltpu.VMEM),
+            pl.BlockSpec(memory_space=pl.ANY),
+        ],
+        out_specs=pl.BlockSpec(memory_space=pltpu.VMEM),
+        scratch_shapes=[
+            pltpu.VMEM((768, 1024), bf16),
+            pltpu.VMEM((16, 32, 128), bf16),
+            pltpu.VMEM((16, 32, 128), bf16),
+            pltpu.VMEM((16, 32, 128), bf16),
+            pltpu.VMEM((16, 1, 128), i32),
+            pltpu.VMEM((16, 1, 128), i32),
+            pltpu.VMEM((6, 128, 512), bf16),
+            pltpu.VMEM((128, 768), bf16),
+            pltpu.VMEM((2, 4, 8, 16, 256), f32),
+            pltpu.VMEM((4, 8, 16, 256), f32),
+            pltpu.VMEM((4, 16, 1152), i16),
+            pltpu.VMEM((4, 16, 1152), i16),
+            pltpu.VMEM((4, 16, 1152), i16),
+            pltpu.VMEM((4, 16, 1152), i16),
+            dma(()), dma((16,)), dma((16,)), dma((16,)), dma((16,)), dma((16,)), dma((16,)),
+            dma((4,)), dma((4,)), dma((4,)), dma((4,)), dma((4,)), dma((4,)),
+        ],
+        compiler_params=pltpu.CompilerParams(
+            collective_id=0, has_side_effects=True, vmem_limit_bytes=24 * 1024 * 1024
+        ),
+        name="ladder",
+    )(tile_block, tile_index, amplitudes.reshape(rows * 16, 128), integrals)
+
+
 def solution(mesh):
-    return jax.shard_map(
-        local,
-        mesh=mesh,
-        in_specs=(P("own", "grp", None), P("own", "grp"), P("own"), P("own")),
-        out_specs=P("own", "grp"),
-        check_vma=False,
-    )
+    count = (mesh.shape["grp"], mesh.shape["own"])
+
+    def run(amplitudes, integrals, tile_block, tile_index):
+        sizes = amplitudes.shape + integrals.shape
+        small = count == (2, 16) and sizes == (192, 32, 128, 12288, 2048)
+        return jax.shard_map(
+            fused if small else local,
+            mesh=mesh,
+            in_specs=(P("own", "grp", None), P("own", "grp"), P("own"), P("own")),
+            out_specs=P("own", "grp"),
+            check_vma=False,
+        )(amplitudes, integrals, tile_block, tile_index)
+
+    return run

time: 109 us -> 31.2 us (0.29)
  the two profiles are of different devices: /device:TPU:0 before, /device:TPU:1 now
where the time goes in v1:
time: 31.2 us; the launch traced here: 31 us
  Pallas kernels  26.8 us (86%)
  local copies, waits for them, and re-layouts  4.15 us (13%)
    pallas_call x1, Pallas kernels, fused(): pl.pallas_call(kernel, out_shape=jax.ShapeDtypeStruct((16, 1024), f32), i...  26.8 us
    unnamed x9, local copies, waits for them, and re-layouts  4.15 us

profile of v1, /device:TPU:1, one launch (start us, length us, event | category | flops | bytes accessed | tf_op | source)
XLA Modules:
  0.0 31.0 jit_solution(16515663125125077106)
XLA Ops:
  0.0 0.0 copy-start
  0.0 1.4 %copy-done = bf16[768,1024]{1,0:T(8,128)(2,1)S(1)} copy-done((bf16[768,1024]{1,0:T(8,128)(2,1)S(1)}, bf16[768,1024]{1,0:T(8,128)(2,1)}, u32[]{:S(2)}) %copy-start) | copy-done | bytes 1572888
  1.4 0.0 copy-start.1
  1.4 0.8 %copy-done.1 = bf16[12,16,128]{2,1,0:T(8,128)(2,1)S(1)} copy-done((bf16[12,16,128]{2,1,0:T(8,128)(2,1)S(1)}, bf16[12,16,128]{2,1,0:T(8,128)(2,1)}, u32[]{:S(2)}) %copy-start.1) | copy-done | bytes 49176
  2.2 0.0 copy-start.2
  2.2 0.7 %copy-done.2 = s32[12]{0:T(128)S(1)} copy-done((s32[12]{0:T(128)S(1)}, s32[12]{0:T(128)}, u32[]{:S(2)}) %copy-start.2) | copy-done | bytes 72
  2.9 0.0 copy-start.3
  2.9 0.7 %copy-done.3 = s32[12]{0:T(128)S(1)} copy-done((s32[12]{0:T(128)S(1)}, s32[12]{0:T(128)}, u32[]{:S(2)}) %copy-start.3) | copy-done | bytes 72
  3.5 26.8 %ladder.1 = f32[16,1024]{1,0:T(8,128)S(1)} custom-call(s32[12]{0:T(128)S(1)} %copy-done.2, s32[12]{0:T(128)S(1)} %copy-done.3, bf16[192,128]{1,0:T(8,128)(2,1)S(1)} %bitcast.1, bf16[768,1024]{1,0:T(8,128)(2,1)S(1)} %copy-done), custom_call_target="tpu_custom_call" | custom-call | tf_op jit(solution)/shard_map/ladder/pallas_call | solution.py:275
  30.3 0.6 %copy.6 = f32[16,1024]{1,0:T(8,128)} copy(f32[16,1024]{1,0:T(8,128)S(1)} %ladder.1) | data formatting | bytes 131072
Async XLA Ops:
  0.0 1.4 %copy-start = (bf16[768,1024]{1,0:T(8,128)(2,1)S(1)}, bf16[768,1024]{1,0:T(8,128)(2,1)}, u32[]{:S(2)}) copy-start(bf16[768,1024]{1,0:T(8,128)(2,1)} %int_hbm.1) | copy-start | bytes 4718596
  1.4 0.8 %copy-start.1 = (bf16[12,16,128]{2,1,0:T(8,128)(2,1)S(1)}, bf16[12,16,128]{2,1,0:T(8,128)(2,1)}, u32[]{:S(2)}) copy-start(bf16[12,16,128]{2,1,0:T(8,128)(2,1)} %param.4) | copy-start | bytes 147460
  2.2 0.7 %copy-start.2 = (s32[12]{0:T(128)S(1)}, s32[12]{0:T(128)}, u32[]{:S(2)}) copy-start(s32[12]{0:T(128)} %block_ref.1) | copy-start | bytes 148
  2.9 0.7 %copy-start.3 = (s32[12]{0:T(128)S(1)}, s32[12]{0:T(128)}, u32[]{:S(2)}) copy-start(s32[12]{0:T(128)} %index_ref.1) | copy-start | bytes 148

commit v2 on v1

--- a/solution.py
+++ b/solution.py
@@ -74,10 +74,10 @@
 
 
 def kernel(
-    block_ref, index_ref, amp_ref, int_hbm, out_ref,
-    ints, sends, recvs, others, key_out, key_in, pick, lhs, prod, sib,
+    block_hbm, index_hbm, amp_hbm, int_hbm, out_ref,
+    block_ref, index_ref, amp_ref, ints, sends, recvs, others, key_out, key_in, pick, lhs, prod, sib,
     x_out, x_in, z_out, z_in,
-    int_sem, tile_ss, tile_rs, key_ss, key_rs, fwd_ss, fwd_rs,
+    int_sem, amp_sem, block_sem, index_sem, tile_ss, tile_rs, key_ss, key_rs, fwd_ss, fwd_rs,
     core_ss, core_rs, x_ss, x_rs, z_ss, z_rs,
 ):
     n = 16
@@ -91,12 +91,21 @@
     sibling = me + 1 - 2 * core
     across = me + 2 - 4 * x
 
+    load_index = pltpu.make_async_copy(index_hbm, index_ref, index_sem)
+    load_block = pltpu.make_async_copy(block_hbm, block_ref, block_sem)
+    load_amp = pltpu.make_async_copy(amp_hbm, amp_ref, amp_sem)
     load = pltpu.make_async_copy(int_hbm, ints, int_sem)
-    load.start()
+    load_index.start()
+    load_block.start()
+    load_amp.start()
     barrier = pltpu.get_barrier_semaphore()
     for d in range(1, n):
         pl.semaphore_signal(barrier, inc=1, device_id={"own": lax.rem(me + d, n)}, device_id_type=MESH)
     pl.semaphore_signal(barrier, inc=1, device_id={"grp": 1 - g}, device_id_type=MESH)
+
+    load.start()
+    load_index.wait()
+    load_block.wait()
 
     owner, rank, key = [], [], []
     for r in range(rows):
@@ -124,6 +133,7 @@
     place = jnp.zeros((1, rows * 16), jnp.int32)
     for r in range(rows):
         place = jnp.where(col // 16 == r, (owner[r] * 2 + rank[r]) * 16 + lax.rem(col, 16), place)
+    load_amp.wait()
     amp = amp_ref[...]
     for part in range(4):
         row = lax.broadcasted_iota(jnp.int32, (128, rows * 16), 0) + part * 128
@@ -147,9 +157,9 @@
             device_id={"own": to}, device_id_type=MESH,
         )
 
-    def forward(s):
-        return pltpu.make_async_remote_copy(
-            recvs.at[s], others.at[s], fwd_ss.at[s], fwd_rs.at[s],
+    def forward(j):
+        return pltpu.make_async_remote_copy(
+            recvs.at[pl.ds(j * 4, 4)], others.at[pl.ds(j * 4, 4)], fwd_ss.at[j], fwd_rs.at[j],
             device_id={"grp": 1 - g}, device_id_type=MESH,
         )
 
@@ -157,7 +167,6 @@
         key_copy(lax.rem(me + d, n)).start()
     for d in ORDER:
         tile_copy(lax.rem(me + d, n)).start()
-    forward(me).start()
 
     def arrived(s, buffer, sem):
         return pltpu.make_async_remote_copy(
@@ -173,19 +182,22 @@
     target = jnp.concatenate(targets, axis=1)
     for t in range(tile_dev):
         row = lax.broadcasted_iota(jnp.int32, (128, 512), 0) + (t * 128 + 1)
-        pick[t] = jnp.where(row == target, 1.0, 0.0).astype(jnp.bfloat16)
-
-    for d in reversed(ORDER):
-        s = lax.rem(me + n - d, n)
-        arrived(s, recvs, tile_rs).wait_recv()
-        forward(s).start()
+        pick[t * 128 : (t + 1) * 128, :] = jnp.where(row == target, 1.0, 0.0).astype(jnp.bfloat16)
+
+    for dz in (0, 1, 3, 2):
+        j = lax.rem(z + dz, 4)
+        for w in range(4):
+            if dz or w:
+                arrived(j * 4 + lax.rem(me + w, 4), recvs, tile_rs).wait_recv()
+        forward(j).start()
+
+    mine_first = core == g
 
     def half(h, source):
         tiles = source[...].reshape(512, 128)
+        got = jnp.dot(pick[...], tiles, preferred_element_type=jnp.float32).astype(jnp.bfloat16)
         for t in range(tile_dev):
-            lhs[:, t * 128 : (t + 1) * 128] = jnp.dot(
-                pick[t], tiles, preferred_element_type=jnp.float32
-            ).astype(jnp.bfloat16)
+            lhs[:, t * 128 : (t + 1) * 128] = got[t * 128 : (t + 1) * 128]
         if h == 0:
             load.wait()
         for k in range(4):
@@ -193,29 +205,20 @@
                 lhs[...], ints[:, k * 256 : (k + 1) * 256], preferred_element_type=jnp.float32
             ).reshape(8, 16, 256)
 
+            @pl.when(mine_first == (h == 1))
+            def _():
+                core_copy(h, k).start()
+
     def core_copy(h, k):
         return pltpu.make_async_remote_copy(
             prod.at[h, k], sib.at[k], core_ss.at[k], core_rs.at[k],
             device_id={"own": sibling}, device_id_type=MESH,
         )
 
-    mine_first = core == g
-
     half(0, recvs)
-
-    @pl.when(jnp.logical_not(mine_first))
-    def _():
-        for k in range(4):
-            core_copy(0, k).start()
-
-    for d in range(n):
-        arrived(lax.rem(me + d, n), others, fwd_rs).wait_recv()
+    for j in range(4):
+        forward(j).wait_recv()
     half(1, others)
-
-    @pl.when(mine_first)
-    def _():
-        for k in range(4):
-            core_copy(1, k).start()
 
     for k in range(4):
         core_copy(0, k).wait_recv()
@@ -258,8 +261,8 @@
         to = lax.rem(me + d, n)
         key_copy(to).wait_send()
         tile_copy(to).wait_send()
-    for s in range(n):
-        forward(s).wait_send()
+    for j in range(4):
+        forward(j).wait_send()
     for k in range(4):
         core_copy(0, k).wait_send()
     for dz in range(4):
@@ -276,20 +279,23 @@
         kernel,
         out_shape=jax.ShapeDtypeStruct((16, 1024), f32),
         in_specs=[
-            pl.BlockSpec(memory_space=pltpu.SMEM),
-            pl.BlockSpec(memory_space=pltpu.SMEM),
-            pl.BlockSpec(memory_space=pltpu.VMEM),
+            pl.BlockSpec(memory_space=pl.ANY),
+            pl.BlockSpec(memory_space=pl.ANY),
+            pl.BlockSpec(memory_space=pl.ANY),
             pl.BlockSpec(memory_space=pl.ANY),
         ],
         out_specs=pl.BlockSpec(memory_space=pltpu.VMEM),
         scratch_shapes=[
+            pltpu.SMEM((rows,), i32),
+            pltpu.SMEM((rows,), i32),
+            pltpu.VMEM((rows * 16, 128), bf16),
             pltpu.VMEM((768, 1024), bf16),
             pltpu.VMEM((16, 32, 128), bf16),
             pltpu.VMEM((16, 32, 128), bf16),
             pltpu.VMEM((16, 32, 128), bf16),
             pltpu.VMEM((16, 1, 128), i32),
             pltpu.VMEM((16, 1, 128), i32),
-            pltpu.VMEM((6, 128, 512), bf16),
+            pltpu.VMEM((768, 512), bf16),
             pltpu.VMEM((128, 768), bf16),
             pltpu.VMEM((2, 4, 8, 16, 256), f32),
             pltpu.VMEM((4, 8, 16, 256), f32),
@@ -297,11 +303,12 @@
             pltpu.VMEM((4, 16, 1152), i16),
             pltpu.VMEM((4, 16, 1152), i16),
             pltpu.VMEM((4, 16, 1152), i16),
-            dma(()), dma((16,)), dma((16,)), dma((16,)), dma((16,)), dma((16,)), dma((16,)),
+            dma(()), dma(()), dma(()), dma(()),
+            dma((16,)), dma((16,)), dma((16,)), dma((16,)), dma((4,)), dma((4,)),
             dma((4,)), dma((4,)), dma((4,)), dma((4,)), dma((4,)), dma((4,)),
         ],
         compiler_params=pltpu.CompilerParams(
-            collective_id=0, has_side_effects=True, vmem_limit_bytes=24 * 1024 * 1024
+            collective_id=0, has_side_effects=True, vmem_limit_bytes=60 * 1024 * 1024
         ),
         name="ladder",
     )(tile_block, tile_index, amplitudes.reshape(rows * 16, 128), integrals)

time: 31.2 us -> 28.7 us (0.920)
  local copies, waits for them, and re-layouts: 4.15 us -> 1.47 us
    unnamed x9 -> x1, local copies, waits for them, and re-layouts: 4.15 us -> 1.47 us
where the time goes in v2:
time: 28.7 us; the launch traced here: 28.4 us
  Pallas kernels  26.9 us (94%)
  local copies, waits for them, and re-layouts  1.47 us (5%)
    pallas_call x1, Pallas kernels, fused(): pl.pallas_call(kernel, out_shape=jax.ShapeDtypeStruct((16, 1024), f32), i...  26.9 us
    unnamed x1, local copies, waits for them, and re-layouts  1.47 us

profile of v2, /device:TPU:1, one launch (start us, length us, event | category | flops | bytes accessed | tf_op | source)
XLA Modules:
  0.0 28.4 jit_solution(4840493317662921321)
XLA Ops:
  0.0 26.9 %ladder.1 = f32[16,1024]{1,0:T(8,128)} custom-call(s32[12]{0:T(128)} %block_hbm.1, s32[12]{0:T(128)} %index_hbm.1, bf16[192,128]{1,0:T(8,128)(2,1)} %bitcast.1, bf16[768,1024]{1,0:T(8,128)(2,1)} %int_hbm.1), custom_call_target="tpu_custom_call" | custom-call | tf_op jit(solution)/shard_map/ladder/pallas_call | solution.py:278
  26.9 1.5 %copy.6 = f32[16,1024]{1,0:T(8,128)} copy(f32[16,1024]{1,0:T(8,128)} %ladder.1) | data formatting | bytes 131072

commit v3 on v2

--- a/solution.py
+++ b/solution.py
@@ -11,7 +11,6 @@
 CAP = 2
 MESH = pl.DeviceIdType.MESH
 ORDER = (8, 7, 9, 6, 10, 5, 11, 4, 12, 3, 13, 2, 14, 1, 15)
-ZORDER = (2, 1, 3, 0)
 
 
 def local(amplitudes, integrals, tile_block, tile_index):
@@ -191,71 +190,88 @@
                 arrived(j * 4 + lax.rem(me + w, 4), recvs, tile_rs).wait_recv()
         forward(j).start()
 
-    mine_first = core == g
-
-    def half(h, source):
+    def place(source):
         tiles = source[...].reshape(512, 128)
         got = jnp.dot(pick[...], tiles, preferred_element_type=jnp.float32).astype(jnp.bfloat16)
         for t in range(tile_dev):
             lhs[:, t * 128 : (t + 1) * 128] = got[t * 128 : (t + 1) * 128]
-        if h == 0:
-            load.wait()
+
+    def core_copy(h, k):
+        return pltpu.make_async_remote_copy(
+            prod.at[h, k, pl.ds(4 * (1 - core), 4)], sib.at[h, k], core_ss.at[h, k], core_rs.at[h, k],
+            device_id={"own": sibling}, device_id_type=MESH,
+        )
+
+    def multiply(h):
         for k in range(4):
             prod[h, k] = jnp.dot(
                 lhs[...], ints[:, k * 256 : (k + 1) * 256], preferred_element_type=jnp.float32
             ).reshape(8, 16, 256)
-
-            @pl.when(mine_first == (h == 1))
+            core_copy(h, k).start()
+
+    def chip_sum(h, b):
+        return jnp.concatenate(
+            [prod[h, k, 4 * core + b] + sib[h, k, b] for k in range(4)], axis=1
+        )
+
+    def x_copy(h, j):
+        return pltpu.make_async_remote_copy(
+            x_out.at[h, j], x_in.at[h, j], x_ss.at[h, j], x_rs.at[h, j],
+            device_id={"own": across}, device_id_type=MESH,
+        )
+
+    def z_copy(h, j):
+        target = 4 * (2 * core + j) + 2 * x + (g if h == 0 else 1 - g)
+        return pltpu.make_async_remote_copy(
+            z_out.at[h, j], z_in.at[z], z_ss.at[h, j], z_rs.at[z],
+            device_id={"own": target}, device_id_type=MESH,
+        )
+
+    def stays(h, j):
+        return jnp.logical_and(z == 2 * core + j, core == (g if h == 0 else 1 - g))
+
+    def x_phase(h):
+        for k in range(4):
+            core_copy(h, k).wait_recv()
+        for j in range(2):
+            x_out[h, j] = encode(chip_sum(h, 2 * j + 1 - x))
+            x_copy(h, j).start()
+
+    def z_phase(h):
+        for j in range(2):
+            x_copy(h, j).wait_recv()
+            total = chip_sum(h, 2 * j + x) + decode(x_in[h, j])
+
+            @pl.when(stays(h, j))
             def _():
-                core_copy(h, k).start()
-
-    def core_copy(h, k):
-        return pltpu.make_async_remote_copy(
-            prod.at[h, k], sib.at[k], core_ss.at[k], core_rs.at[k],
-            device_id={"own": sibling}, device_id_type=MESH,
-        )
-
-    half(0, recvs)
+                out_ref[...] = total
+
+            @pl.when(jnp.logical_not(stays(h, j)))
+            def _():
+                z_out[h, j] = encode(total)
+                z_copy(h, j).start()
+
+    place(recvs)
+    load.wait()
+    multiply(0)
     for j in range(4):
         forward(j).wait_recv()
-    half(1, others)
-
-    for k in range(4):
-        core_copy(0, k).wait_recv()
-    keep = lax.rem(core + g, 2)
-
-    def chip_sum(b):
-        return jnp.concatenate([prod[keep, k, b] + sib[k, b] for k in range(4)], axis=1)
-
-    def x_copy(dz):
-        return pltpu.make_async_remote_copy(
-            x_out.at[dz], x_in.at[dz], x_ss.at[dz], x_rs.at[dz],
-            device_id={"own": across}, device_id_type=MESH,
-        )
-
-    def z_copy(dz):
-        return pltpu.make_async_remote_copy(
-            z_out.at[dz], z_in.at[dz], z_ss.at[dz], z_rs.at[dz],
-            device_id={"own": lax.rem(me + 4 * dz, n)}, device_id_type=MESH,
-        )
-
-    for dz in ZORDER:
-        to_z = lax.rem(z + dz, 4)
-        x_out[dz] = encode(chip_sum(to_z * 2 + 1 - x))
-        x_copy(dz).start()
-    for dz in ZORDER:
-        to_z = lax.rem(z + dz, 4)
-        total = chip_sum(to_z * 2 + x)
-        x_copy(dz).wait_recv()
-        total = total + decode(x_in[dz])
-        if dz:
-            z_out[dz] = encode(total)
-            z_copy(dz).start()
-        else:
-            out_ref[...] = total
+    place(others)
+    x_phase(0)
+    multiply(1)
+    z_phase(0)
+    x_phase(1)
+    z_phase(1)
+
+    @pl.when(z // 2 != core)
+    def _():
+        arrived(z, z_in, z_rs).wait_recv()
+        out_ref[...] = decode(z_in[z])
+
     for dz in (1, 3, 2):
-        z_copy(dz).wait_recv()
-        out_ref[...] += decode(z_in[dz])
+        source = lax.rem(z + dz, 4)
+        arrived(source, z_in, z_rs).wait_recv()
+        out_ref[...] += decode(z_in[source])
 
     for d in ORDER:
         to = lax.rem(me + d, n)
@@ -263,12 +279,15 @@
         tile_copy(to).wait_send()
     for j in range(4):
         forward(j).wait_send()
-    for k in range(4):
-        core_copy(0, k).wait_send()
-    for dz in range(4):
-        x_copy(dz).wait_send()
-        if dz:
-            z_copy(dz).wait_send()
+    for h in range(2):
+        for k in range(4):
+            core_copy(h, k).wait_send()
+        for j in range(2):
+            x_copy(h, j).wait_send()
+
+            @pl.when(jnp.logical_not(stays(h, j)))
+            def _():
+                z_copy(h, j).wait_send()
 
 
 def fused(amplitudes, integrals, tile_block, tile_index):
@@ -298,14 +317,14 @@
             pltpu.VMEM((768, 512), bf16),
             pltpu.VMEM((128, 768), bf16),
             pltpu.VMEM((2, 4, 8, 16, 256), f32),
-            pltpu.VMEM((4, 8, 16, 256), f32),
-            pltpu.VMEM((4, 16, 1152), i16),
-            pltpu.VMEM((4, 16, 1152), i16),
-            pltpu.VMEM((4, 16, 1152), i16),
+            pltpu.VMEM((2, 4, 4, 16, 256), f32),
+            pltpu.VMEM((2, 2, 16, 1152), i16),
+            pltpu.VMEM((2, 2, 16, 1152), i16),
+            pltpu.VMEM((2, 2, 16, 1152), i16),
             pltpu.VMEM((4, 16, 1152), i16),
             dma(()), dma(()), dma(()), dma(()),
             dma((16,)), dma((16,)), dma((16,)), dma((16,)), dma((4,)), dma((4,)),
-            dma((4,)), dma((4,)), dma((4,)), dma((4,)), dma((4,)), dma((4,)),
+            dma((2, 4)), dma((2, 4)), dma((2, 2)), dma((2, 2)), dma((2, 2)), dma((4,)),
         ],
         compiler_params=pltpu.CompilerParams(
             collective_id=0, has_side_effects=True, vmem_limit_bytes=60 * 1024 * 1024

time: 28.7 us -> 29 us (1.010)
  Pallas kernels: 26.9 us -> 27.4 us
    pallas_call x1, Pallas kernels: 26.9 us -> 27.4 us  [fused(): pl.pallas_call(kernel, out_shape=jax.ShapeDtypeStruct((16, 1024), f32), i...]
where the time goes in v3:
time: 29 us; the launch traced here: 28.8 us
  Pallas kernels  27.4 us (94%)
  local copies, waits for them, and re-layouts  1.47 us (5%)
    pallas_call x1, Pallas kernels, fused(): pl.pallas_call(kernel, out_shape=jax.ShapeDtypeStruct((16, 1024), f32), i...  27.4 us
    unnamed x1, local copies, waits for them, and re-layouts  1.47 us

profile of v3, /device:TPU:1, one launch (start us, length us, event | category | flops | bytes accessed | tf_op | source)
XLA Modules:
  0.0 28.8 jit_solution(7919808068420747921)
XLA Ops:
  0.0 27.4 %ladder.1 = f32[16,1024]{1,0:T(8,128)} custom-call(s32[12]{0:T(128)} %block_hbm.1, s32[12]{0:T(128)} %index_hbm.1, bf16[192,128]{1,0:T(8,128)(2,1)} %bitcast.1, bf16[768,1024]{1,0:T(8,128)(2,1)} %int_hbm.1), custom_call_target="tpu_custom_call" | custom-call | tf_op jit(solution)/shard_map/ladder/pallas_call | solution.py:297
  27.4 1.5 %copy.6 = f32[16,1024]{1,0:T(8,128)} copy(f32[16,1024]{1,0:T(8,128)} %ladder.1) | data formatting | bytes 131072

commit v4 on v3

--- a/solution.py
+++ b/solution.py
@@ -10,7 +10,13 @@
 NB = 8
 CAP = 2
 MESH = pl.DeviceIdType.MESH
-ORDER = (8, 7, 9, 6, 10, 5, 11, 4, 12, 3, 13, 2, 14, 1, 15)
+
+
+def loop(count):
+    def run(body):
+        lax.fori_loop(0, count, lambda i, carry: (body(i), carry)[1], 0)
+
+    return run
 
 
 def local(amplitudes, integrals, tile_block, tile_index):
@@ -74,7 +80,7 @@
 
 def kernel(
     block_hbm, index_hbm, amp_hbm, int_hbm, out_ref,
-    block_ref, index_ref, amp_ref, ints, sends, recvs, others, key_out, key_in, pick, lhs, prod, sib,
+    block_ref, index_ref, amp_ref, ints, sends, tiles, key_out, key_in, pick, lhs, prod, sib,
     x_out, x_in, z_out, z_in,
     int_sem, amp_sem, block_sem, index_sem, tile_ss, tile_rs, key_ss, key_rs, fwd_ss, fwd_rs,
     core_ss, core_rs, x_ss, x_rs, z_ss, z_rs,
@@ -98,8 +104,11 @@
     load_block.start()
     load_amp.start()
     barrier = pltpu.get_barrier_semaphore()
-    for d in range(1, n):
-        pl.semaphore_signal(barrier, inc=1, device_id={"own": lax.rem(me + d, n)}, device_id_type=MESH)
+
+    @loop(n - 1)
+    def _(i):
+        pl.semaphore_signal(barrier, inc=1, device_id={"own": lax.rem(me + i + 1, n)}, device_id_type=MESH)
+
     pl.semaphore_signal(barrier, inc=1, device_id={"grp": 1 - g}, device_id_type=MESH)
 
     load.start()
@@ -134,12 +143,15 @@
         place = jnp.where(col // 16 == r, (owner[r] * 2 + rank[r]) * 16 + lax.rem(col, 16), place)
     load_amp.wait()
     amp = amp_ref[...]
-    for part in range(4):
-        row = lax.broadcasted_iota(jnp.int32, (128, rows * 16), 0) + part * 128
-        hot = jnp.where(row == place, 1.0, 0.0).astype(jnp.bfloat16)
+
+    @loop(4)
+    def _(part):
+        row = lax.broadcasted_iota(jnp.int32, (128, rows * 16), 0)
+        hot = jnp.where(row == place - part * 128, 1.0, 0.0).astype(jnp.bfloat16)
         got = jnp.dot(hot, amp, preferred_element_type=jnp.float32).astype(jnp.bfloat16)
         sends[pl.ds(part * 4, 4)] = got.reshape(4, 32, 128)
-    recvs[me] = sends[me]
+
+    tiles[0, me] = sends[me]
     key_in[me] = key_out[me]
 
     pl.semaphore_wait(barrier, n)
@@ -152,20 +164,27 @@
 
     def tile_copy(to):
         return pltpu.make_async_remote_copy(
-            sends.at[to], recvs.at[me], tile_ss.at[to], tile_rs.at[me],
+            sends.at[to], tiles.at[0, me], tile_ss.at[to], tile_rs.at[me],
             device_id={"own": to}, device_id_type=MESH,
         )
 
     def forward(j):
         return pltpu.make_async_remote_copy(
-            recvs.at[pl.ds(j * 4, 4)], others.at[pl.ds(j * 4, 4)], fwd_ss.at[j], fwd_rs.at[j],
+            tiles.at[0, pl.ds(j * 4, 4)], tiles.at[1, pl.ds(j * 4, 4)], fwd_ss.at[j], fwd_rs.at[j],
             device_id={"grp": 1 - g}, device_id_type=MESH,
         )
 
-    for d in ORDER:
-        key_copy(lax.rem(me + d, n)).start()
-    for d in ORDER:
-        tile_copy(lax.rem(me + d, n)).start()
+    def others(body):
+        @loop(n)
+        def _(i):
+            to = lax.rem(z + 2 + i // 4, 4) * 4 + lax.rem(me + i, 4)
+
+            @pl.when(to != me)
+            def _():
+                body(to)
+
+    others(lambda to: key_copy(to).start())
+    others(lambda to: tile_copy(to).start())
 
     def arrived(s, buffer, sem):
         return pltpu.make_async_remote_copy(
@@ -173,28 +192,39 @@
             device_id={"own": sibling}, device_id_type=MESH,
         )
 
-    for d in ORDER:
-        arrived(lax.rem(me + n - d, n), key_in, key_rs).wait_recv()
+    others(lambda s: arrived(s, key_in, key_rs).wait_recv())
     targets = [
         key_in[4 * j] + key_in[4 * j + 1] + key_in[4 * j + 2] + key_in[4 * j + 3] for j in range(4)
     ]
     target = jnp.concatenate(targets, axis=1)
-    for t in range(tile_dev):
-        row = lax.broadcasted_iota(jnp.int32, (128, 512), 0) + (t * 128 + 1)
-        pick[t * 128 : (t + 1) * 128, :] = jnp.where(row == target, 1.0, 0.0).astype(jnp.bfloat16)
-
-    for dz in (0, 1, 3, 2):
-        j = lax.rem(z + dz, 4)
-        for w in range(4):
-            if dz or w:
-                arrived(j * 4 + lax.rem(me + w, 4), recvs, tile_rs).wait_recv()
+
+    @loop(tile_dev)
+    def _(t):
+        row = lax.broadcasted_iota(jnp.int32, (128, 512), 0)
+        pick[pl.ds(pl.multiple_of(t * 128, 128), 128), :] = jnp.where(
+            row == target - (t * 128 + 1), 1.0, 0.0
+        ).astype(jnp.bfloat16)
+
+    @loop(4)
+    def _(i):
+        j = lax.rem(z + i, 4)
+
+        @loop(4)
+        def _(w):
+            s = j * 4 + w
+
+            @pl.when(s != me)
+            def _():
+                arrived(s, tiles.at[0], tile_rs).wait_recv()
+
         forward(j).start()
 
-    def place(source):
-        tiles = source[...].reshape(512, 128)
-        got = jnp.dot(pick[...], tiles, preferred_element_type=jnp.float32).astype(jnp.bfloat16)
+    def place(h):
+        slots = tiles[h].reshape(512, 128)
         for t in range(tile_dev):
-            lhs[:, t * 128 : (t + 1) * 128] = got[t * 128 : (t + 1) * 128]
+            lhs[:, t * 128 : (t + 1) * 128] = jnp.dot(
+                pick[t * 128 : (t + 1) * 128, :], slots, preferred_element_type=jnp.float32
+            ).astype(jnp.bfloat16)
 
     def core_copy(h, k):
         return pltpu.make_async_remote_copy(
@@ -203,9 +233,11 @@
         )
 
     def multiply(h):
-        for k in range(4):
+        @loop(4)
+        def _(k):
+            cols = pl.ds(pl.multiple_of(k * 256, 256), 256)
             prod[h, k] = jnp.dot(
-                lhs[...], ints[:, k * 256 : (k + 1) * 256], preferred_element_type=jnp.float32
+                lhs[...], ints[:, cols], preferred_element_type=jnp.float32
             ).reshape(8, 16, 256)
             core_copy(h, k).start()
 
@@ -221,68 +253,85 @@
         )
 
     def z_copy(h, j):
-        target = 4 * (2 * core + j) + 2 * x + (g if h == 0 else 1 - g)
+        target = 4 * (2 * core + j) + 2 * x + lax.rem(g + h, 2)
         return pltpu.make_async_remote_copy(
             z_out.at[h, j], z_in.at[z], z_ss.at[h, j], z_rs.at[z],
             device_id={"own": target}, device_id_type=MESH,
         )
 
     def stays(h, j):
-        return jnp.logical_and(z == 2 * core + j, core == (g if h == 0 else 1 - g))
+        return jnp.logical_and(z == 2 * core + j, core == lax.rem(g + h, 2))
 
     def x_phase(h):
         for k in range(4):
             core_copy(h, k).wait_recv()
-        for j in range(2):
+
+        @loop(2)
+        def _(j):
             x_out[h, j] = encode(chip_sum(h, 2 * j + 1 - x))
             x_copy(h, j).start()
 
-    def z_phase(h):
-        for j in range(2):
-            x_copy(h, j).wait_recv()
-            total = chip_sum(h, 2 * j + x) + decode(x_in[h, j])
-
-            @pl.when(stays(h, j))
+    def z_phase(h, j):
+        x_copy(h, j).wait_recv()
+        total = chip_sum(h, 2 * j + x) + decode(x_in[h, j])
+
+        @pl.when(stays(h, j))
+        def _():
+            out_ref[...] = total
+
+        @pl.when(jnp.logical_not(stays(h, j)))
+        def _():
+            z_out[h, j] = encode(total)
+            z_copy(h, j).start()
+
+    load.wait()
+
+    @loop(3)
+    def _(i):
+        @pl.when(i < 2)
+        def _():
+            @pl.when(i == 1)
             def _():
-                out_ref[...] = total
-
-            @pl.when(jnp.logical_not(stays(h, j)))
-            def _():
-                z_out[h, j] = encode(total)
-                z_copy(h, j).start()
-
-    place(recvs)
-    load.wait()
-    multiply(0)
-    for j in range(4):
-        forward(j).wait_recv()
-    place(others)
-    x_phase(0)
-    multiply(1)
-    z_phase(0)
-    x_phase(1)
-    z_phase(1)
+                for j in range(4):
+                    forward(j).wait_recv()
+
+            place(i)
+            multiply(i)
+
+        @pl.when(i > 0)
+        def _():
+            x_phase(i - 1)
+
+    @loop(4)
+    def _(i):
+        z_phase(i // 2, lax.rem(i, 2))
 
     @pl.when(z // 2 != core)
     def _():
         arrived(z, z_in, z_rs).wait_recv()
         out_ref[...] = decode(z_in[z])
 
-    for dz in (1, 3, 2):
-        source = lax.rem(z + dz, 4)
+    @loop(3)
+    def _(i):
+        source = lax.rem(z + i + 1, 4)
         arrived(source, z_in, z_rs).wait_recv()
         out_ref[...] += decode(z_in[source])
 
-    for d in ORDER:
-        to = lax.rem(me + d, n)
+    @others
+    def _(to):
         key_copy(to).wait_send()
         tile_copy(to).wait_send()
+
     for j in range(4):
         forward(j).wait_send()
-    for h in range(2):
+
+    @loop(2)
+    def _(h):
         for k in range(4):
             core_copy(h, k).wait_send()
-        for j in range(2):
+
+        @loop(2)
+        def _(j):
             x_copy(h, j).wait_send()
 
             @pl.when(jnp.logical_not(stays(h, j)))
@@ -310,8 +359,7 @@
             pltpu.VMEM((rows * 16, 128), bf16),
             pltpu.VMEM((768, 1024), bf16),
             pltpu.VMEM((16, 32, 128), bf16),
-            pltpu.VMEM((16, 32, 128), bf16),
-            pltpu.VMEM((16, 32, 128), bf16),
+            pltpu.VMEM((2, 16, 32, 128), bf16),
             pltpu.VMEM((16, 1, 128), i32),
             pltpu.VMEM((16, 1, 128), i32),
             pltpu.VMEM((768, 512), bf16),

time: 29 us -> 28.4 us (0.979)
  Pallas kernels: 27.4 us -> 26.7 us
    pallas_call x1, Pallas kernels: 27.4 us -> 26.7 us  [fused(): pl.pallas_call(kernel, out_shape=jax.ShapeDtypeStruct((16, 1024), f32), i...]
where the time goes in v4:
time: 28.4 us; the launch traced here: 28.2 us
  Pallas kernels  26.7 us (94%)
  local copies, waits for them, and re-layouts  1.47 us (5%)
    pallas_call x1, Pallas kernels, fused(): pl.pallas_call(kernel, out_shape=jax.ShapeDtypeStruct((16, 1024), f32), i...  26.7 us
    unnamed x1, local copies, waits for them, and re-layouts  1.47 us

profile of v4, /device:TPU:1, one launch (start us, length us, event | category | flops | bytes accessed | tf_op | source)
XLA Modules:
  0.0 28.2 jit_solution(14042917226538385302)
XLA Ops:
  0.0 26.7 %ladder.1 = f32[16,1024]{1,0:T(8,128)} custom-call(s32[12]{0:T(128)} %block_hbm.1, s32[12]{0:T(128)} %index_hbm.1, bf16[192,128]{1,0:T(8,128)(2,1)} %bitcast.1, bf16[768,1024]{1,0:T(8,128)(2,1)} %int_hbm.1), custom_call_target="tpu_custom_call" | custom-call | tf_op jit(solution)/shard_map/ladder/pallas_call | solution.py:346
  26.7 1.5 %copy.6 = f32[16,1024]{1,0:T(8,128)} copy(f32[16,1024]{1,0:T(8,128)} %ladder.1) | data formatting | bytes 131072

commit v5 on v4

--- a/solution.py
+++ b/solution.py
@@ -81,9 +81,9 @@
 def kernel(
     block_hbm, index_hbm, amp_hbm, int_hbm, out_ref,
     block_ref, index_ref, amp_ref, ints, sends, tiles, key_out, key_in, pick, lhs, prod, sib,
-    x_out, x_in, z_out, z_in,
+    coded, landed,
     int_sem, amp_sem, block_sem, index_sem, tile_ss, tile_rs, key_ss, key_rs, fwd_ss, fwd_rs,
-    core_ss, core_rs, x_ss, x_rs, z_ss, z_rs,
+    core_ss, core_rs, sum_ss, sum_rs,
 ):
     n = 16
     rows = amp_ref.shape[0] // 16
@@ -91,10 +91,8 @@
     me = lax.axis_index("own")
     g = lax.axis_index("grp")
     core = lax.rem(me, 2)
-    x = lax.rem(me // 2, 2)
     z = me // 4
     sibling = me + 1 - 2 * core
-    across = me + 2 - 4 * x
 
     load_index = pltpu.make_async_copy(index_hbm, index_ref, index_sem)
     load_block = pltpu.make_async_copy(block_hbm, block_ref, block_sem)
@@ -138,19 +136,15 @@
         key_out[o] = keys[o : o + 1, :]
 
     col = lax.broadcasted_iota(jnp.int32, (1, rows * 16), 1)
-    place = jnp.zeros((1, rows * 16), jnp.int32)
+    place_row = jnp.zeros((1, rows * 16), jnp.int32)
     for r in range(rows):
-        place = jnp.where(col // 16 == r, (owner[r] * 2 + rank[r]) * 16 + lax.rem(col, 16), place)
+        place_row = jnp.where(col // 16 == r, (owner[r] * 2 + rank[r]) * 16 + lax.rem(col, 16), place_row)
     load_amp.wait()
     amp = amp_ref[...]
 
-    @loop(4)
-    def _(part):
-        row = lax.broadcasted_iota(jnp.int32, (128, rows * 16), 0)
-        hot = jnp.where(row == place - part * 128, 1.0, 0.0).astype(jnp.bfloat16)
-        got = jnp.dot(hot, amp, preferred_element_type=jnp.float32).astype(jnp.bfloat16)
-        sends[pl.ds(part * 4, 4)] = got.reshape(4, 32, 128)
-
+    row = lax.broadcasted_iota(jnp.int32, (512, rows * 16), 0)
+    hot = jnp.where(row == place_row, 1.0, 0.0).astype(jnp.bfloat16)
+    sends[...] = jnp.dot(hot, amp, preferred_element_type=jnp.float32).astype(jnp.bfloat16).reshape(16, 32, 128)
     tiles[0, me] = sends[me]
     key_in[me] = key_out[me]
 
@@ -221,10 +215,9 @@
 
     def place(h):
         slots = tiles[h].reshape(512, 128)
+        got = jnp.dot(pick[...], slots, preferred_element_type=jnp.float32).astype(jnp.bfloat16)
         for t in range(tile_dev):
-            lhs[:, t * 128 : (t + 1) * 128] = jnp.dot(
-                pick[t * 128 : (t + 1) * 128, :], slots, preferred_element_type=jnp.float32
-            ).astype(jnp.bfloat16)
+            lhs[:, t * 128 : (t + 1) * 128] = got[t * 128 : (t + 1) * 128]
 
     def core_copy(h, k):
         return pltpu.make_async_remote_copy(
@@ -232,90 +225,74 @@
             device_id={"own": sibling}, device_id_type=MESH,
         )
 
-    def multiply(h):
-        @loop(4)
-        def _(k):
-            cols = pl.ds(pl.multiple_of(k * 256, 256), 256)
-            prod[h, k] = jnp.dot(
-                lhs[...], ints[:, cols], preferred_element_type=jnp.float32
-            ).reshape(8, 16, 256)
-            core_copy(h, k).start()
+    def multiply(h, k):
+        cols = pl.ds(pl.multiple_of(k * 256, 256), 256)
+        prod[h, k] = jnp.dot(
+            lhs[...], ints[:, cols], preferred_element_type=jnp.float32
+        ).reshape(8, 16, 256)
 
     def chip_sum(h, b):
         return jnp.concatenate(
             [prod[h, k, 4 * core + b] + sib[h, k, b] for k in range(4)], axis=1
         )
 
-    def x_copy(h, j):
-        return pltpu.make_async_remote_copy(
-            x_out.at[h, j], x_in.at[h, j], x_ss.at[h, j], x_rs.at[h, j],
-            device_id={"own": across}, device_id_type=MESH,
-        )
-
-    def z_copy(h, j):
-        target = 4 * (2 * core + j) + 2 * x + lax.rem(g + h, 2)
-        return pltpu.make_async_remote_copy(
-            z_out.at[h, j], z_in.at[z], z_ss.at[h, j], z_rs.at[z],
-            device_id={"own": target}, device_id_type=MESH,
-        )
-
-    def stays(h, j):
-        return jnp.logical_and(z == 2 * core + j, core == lax.rem(g + h, 2))
-
-    def x_phase(h):
-        for k in range(4):
-            core_copy(h, k).wait_recv()
-
-        @loop(2)
-        def _(j):
-            x_out[h, j] = encode(chip_sum(h, 2 * j + 1 - x))
-            x_copy(h, j).start()
-
-    def z_phase(h, j):
-        x_copy(h, j).wait_recv()
-        total = chip_sum(h, 2 * j + x) + decode(x_in[h, j])
-
-        @pl.when(stays(h, j))
+    def send_to(h, q):
+        return 8 * core + 2 * q + lax.rem(g + h, 2)
+
+    def sum_copy(h, q):
+        return pltpu.make_async_remote_copy(
+            coded.at[h, q], landed.at[me // 2], sum_ss.at[h, q], sum_rs.at[me // 2],
+            device_id={"own": send_to(h, q)}, device_id_type=MESH,
+        )
+
+    def prepare(h, q):
+        total = chip_sum(h, q)
+        coded[h, q] = encode(total)
+        out_ref[...] += jnp.where(send_to(h, q) == me, total, 0.0)
+
+    def send(h, q):
+        @pl.when(send_to(h, q) != me)
         def _():
-            out_ref[...] = total
-
-        @pl.when(jnp.logical_not(stays(h, j)))
+            sum_copy(h, q).start()
+
+    out_ref[...] = jnp.zeros_like(out_ref)
+    load.wait()
+    place(0)
+
+    @loop(4)
+    def _(k):
+        multiply(0, k)
+        core_copy(0, k).start()
+
+    for j in range(4):
+        forward(j).wait_recv()
+    place(1)
+    for k in range(4):
+        core_copy(0, k).wait_recv()
+
+    @loop(4)
+    def _(k):
+        prepare(0, k)
+        multiply(1, k)
+        core_copy(1, k).start()
+        send(0, k)
+
+    for k in range(4):
+        core_copy(1, k).wait_recv()
+
+    @loop(4)
+    def _(k):
+        prepare(1, k)
+        send(1, k)
+
+    @loop(8)
+    def _(i):
+        source = lax.rem(me // 2 + i, 8)
+
+        @pl.when(jnp.logical_or(i > 0, z // 2 != core))
         def _():
-            z_out[h, j] = encode(total)
-            z_copy(h, j).start()
-
-    load.wait()
-
-    @loop(3)
-    def _(i):
-        @pl.when(i < 2)
-        def _():
-            @pl.when(i == 1)
-            def _():
-                for j in range(4):
-                    forward(j).wait_recv()
-
-            place(i)
-            multiply(i)
-
-        @pl.when(i > 0)
-        def _():
-            x_phase(i - 1)
-
-    @loop(4)
-    def _(i):
-        z_phase(i // 2, lax.rem(i, 2))
-
-    @pl.when(z // 2 != core)
-    def _():
-        arrived(z, z_in, z_rs).wait_recv()
-        out_ref[...] = decode(z_in[z])
-
-    @loop(3)
-    def _(i):
-        source = lax.rem(z + i + 1, 4)
-        arrived(source, z_in, z_rs).wait_recv()
-        out_ref[...] += decode(z_in[source])
+            arrived(source, landed, sum_rs).wait_recv()
+            out_ref[...] += decode(landed[source])
 
     @others
     def _(to):
@@ -330,13 +307,11 @@
         for k in range(4):
             core_copy(h, k).wait_send()
 
-        @loop(2)
-        def _(j):
-            x_copy(h, j).wait_send()
-
-            @pl.when(jnp.logical_not(stays(h, j)))
+        @loop(4)
+        def _(q):
+            @pl.when(send_to(h, q) != me)
             def _():
-                z_copy(h, j).wait_send()
+                sum_copy(h, q).wait_send()
 
 
 def fused(amplitudes, integrals, tile_block, tile_index):
@@ -366,13 +341,11 @@
             pltpu.VMEM((128, 768), bf16),
             pltpu.VMEM((2, 4, 8, 16, 256), f32),
             pltpu.VMEM((2, 4, 4, 16, 256), f32),
-            pltpu.VMEM((2, 2, 16, 1152), i16),
-            pltpu.VMEM((2, 2, 16, 1152), i16),
-            pltpu.VMEM((2, 2, 16, 1152), i16),
-            pltpu.VMEM((4, 16, 1152), i16),
+            pltpu.VMEM((2, 4, 16, 1152), i16),
+            pltpu.VMEM((8, 16, 1152), i16),
             dma(()), dma(()), dma(()), dma(()),
             dma((16,)), dma((16,)), dma((16,)), dma((16,)), dma((4,)), dma((4,)),
-            dma((2, 4)), dma((2, 4)), dma((2, 2)), dma((2, 2)), dma((2, 2)), dma((4,)),
+            dma((2, 4)), dma((2, 4)), dma((2, 4)), dma((8,)),
         ],
         compiler_params=pltpu.CompilerParams(
             collective_id=0, has_side_effects=True, vmem_limit_bytes=60 * 1024 * 1024

time: 28.4 us -> 26.1 us (0.919)
  Pallas kernels: 26.7 us -> 24.3 us
    pallas_call x1, Pallas kernels: 26.7 us -> 24.3 us  [fused(): pl.pallas_call(kernel, out_shape=jax.ShapeDtypeStruct((16, 1024), f32), i...]
where the time goes in v5:
time: 26.1 us; the launch traced here: 25.8 us
  Pallas kernels  24.3 us (93%)
  local copies, waits for them, and re-layouts  1.47 us (6%)
    pallas_call x1, Pallas kernels, fused(): pl.pallas_call(kernel, out_shape=jax.ShapeDtypeStruct((16, 1024), f32), i...  24.3 us
    unnamed x1, local copies, waits for them, and re-layouts  1.47 us

profile of v5, /device:TPU:1, one launch (start us, length us, event | category | flops | bytes accessed | tf_op | source)
XLA Modules:
  0.0 25.8 jit_solution(6727050999767913825)
XLA Ops:
  0.0 24.3 %ladder.1 = f32[16,1024]{1,0:T(8,128)} custom-call(s32[12]{0:T(128)} %block_hbm.1, s32[12]{0:T(128)} %index_hbm.1, bf16[192,128]{1,0:T(8,128)(2,1)} %bitcast.1, bf16[768,1024]{1,0:T(8,128)(2,1)} %int_hbm.1), custom_call_target="tpu_custom_call" | custom-call | tf_op jit(solution)/shard_map/ladder/pallas_call | solution.py:321
  24.3 1.5 %copy.6 = f32[16,1024]{1,0:T(8,128)} copy(f32[16,1024]{1,0:T(8,128)} %ladder.1) | data formatting | bytes 131072

commit v6 on v5

--- a/solution.py
+++ b/solution.py
@@ -67,15 +67,22 @@
     parts = [v[:, k * 128 : (k + 1) * 128] for k in range(8)]
     top = functools.reduce(jnp.maximum, [jnp.abs(p) for p in parts])
     expo = jnp.ceil(jnp.log2(jnp.maximum(top, 1e-30)))
-    scale = jnp.exp2(15.0 - expo)
-    coded = [jnp.clip(jnp.round(p * scale), -32767.0, 32767.0) for p in parts] + [expo]
-    return jnp.concatenate(coded, axis=1).astype(jnp.int32).astype(jnp.int16)
+    scale = jnp.exp2(14.0 - expo)
+    low = expo.astype(jnp.int32) + 128
+    coded = [
+        jnp.clip(jnp.round(p * scale), -16383.0, 16383.0).astype(jnp.int32) * 2 + ((low >> k) & 1)
+        for k, p in enumerate(parts)
+    ]
+    return jnp.concatenate(coded, axis=1).astype(jnp.int16)
 
 
 def decode(q):
-    wide = q.astype(jnp.int32).astype(jnp.float32)
-    scale = jnp.exp2(wide[:, 1024:] - 15.0)
-    return jnp.concatenate([wide[:, k * 128 : (k + 1) * 128] * scale for k in range(8)], axis=1)
+    wide = q.astype(jnp.int32)
+    parts = [wide[:, k * 128 : (k + 1) * 128] for k in range(8)]
+    bits = [p & 1 for p in parts]
+    low = functools.reduce(jnp.add, [b << k for k, b in enumerate(bits)])
+    scale = jnp.exp2((low - 143).astype(jnp.float32))
+    return jnp.concatenate([(p - b).astype(jnp.float32) * scale for p, b in zip(parts, bits)], axis=1)
 
 
 def kernel(
@@ -118,7 +125,9 @@
         t = index_ref[r]
         o = t // tile_dev
         owner.append(o)
-        key.append((t - o * tile_dev) * NB + block_ref[r])
+        b = block_ref[r]
+        place_of = (b // 2 % 2) * 4 + (b // 4) * 2 + b % 2
+        key.append((t - o * tile_dev) * NB + place_of)
         earlier = jnp.int32(0)
         for q in range(r):
             earlier = earlier + jnp.where(owner[q] == o, 1, 0)
@@ -237,7 +246,7 @@
         )
 
     def send_to(h, q):
-        return 8 * core + 2 * q + lax.rem(g + h, 2)
+        return 4 * (core + 2 * (q // 2)) + 2 * lax.rem(q, 2) + lax.rem(g + h, 2)
 
     def sum_copy(h, q):
         return pltpu.make_async_remote_copy(
@@ -254,6 +263,9 @@
         @pl.when(send_to(h, q) != me)
         def _():
             sum_copy(h, q).start()
+
+    def turn(k):
+        return lax.rem(k + 2 * (1 - z // 2), 4)
 
     out_ref[...] = jnp.zeros_like(out_ref)
     load.wait()
@@ -272,24 +284,26 @@
 
     @loop(4)
     def _(k):
-        prepare(0, k)
+        q = turn(k)
+        prepare(0, q)
         multiply(1, k)
         core_copy(1, k).start()
-        send(0, k)
+        send(0, q)
 
     for k in range(4):
         core_copy(1, k).wait_recv()
 
     @loop(4)
     def _(k):
-        prepare(1, k)
-        send(1, k)
+        q = turn(k)
+        prepare(1, q)
+        send(1, q)
 
     @loop(8)
     def _(i):
         source = lax.rem(me // 2 + i, 8)
 
-        @pl.when(jnp.logical_or(i > 0, z // 2 != core))
+        @pl.when(jnp.logical_or(i > 0, lax.rem(z, 2) != core))
         def _():
             arrived(source, landed, sum_rs).wait_recv()
             out_ref[...] += decode(landed[source])
@@ -320,7 +334,7 @@
     bf16, f32, i32, i16 = jnp.bfloat16, jnp.float32, jnp.int32, jnp.int16
     return pl.pallas_call(
         kernel,
-        out_shape=jax.ShapeDtypeStruct((16, 1024), f32),
+        out_shape=pltpu.VMEM((16, 1024), f32),
         in_specs=[
             pl.BlockSpec(memory_space=pl.ANY),
             pl.BlockSpec(memory_space=pl.ANY),
@@ -341,14 +355,14 @@
             pltpu.VMEM((128, 768), bf16),
             pltpu.VMEM((2, 4, 8, 16, 256), f32),
             pltpu.VMEM((2, 4, 4, 16, 256), f32),
-            pltpu.VMEM((2, 4, 16, 1152), i16),
-            pltpu.VMEM((8, 16, 1152), i16),
+            pltpu.VMEM((2, 4, 16, 1024), i16),
+            pltpu.VMEM((8, 16, 1024), i16),
             dma(()), dma(()), dma(()), dma(()),
             dma((16,)), dma((16,)), dma((16,)), dma((16,)), dma((4,)), dma((4,)),
             dma((2, 4)), dma((2, 4)), dma((2, 4)), dma((8,)),
         ],
         compiler_params=pltpu.CompilerParams(
-            collective_id=0, has_side_effects=True, vmem_limit_bytes=60 * 1024 * 1024
+            collective_id=0, has_side_effects=True, vmem_limit_bytes=56 * 1024 * 1024
         ),
         name="ladder",
     )(tile_block, tile_index, amplitudes.reshape(rows * 16, 128), integrals)

time: 26.1 us -> 24.1 us (0.923)
  Pallas kernels: 24.3 us -> 23.3 us
  local copies, waits for them, and re-layouts: 1.47 us -> 0.63 us
    pallas_call x1, Pallas kernels: 24.3 us -> 23.3 us  [fused(): pl.pallas_call(kernel, out_shape=pltpu.VMEM((16, 1024), f32), in_specs=[p...]
    unnamed x1, local copies, waits for them, and re-layouts: 1.47 us -> 0.63 us
where the time goes in v6:
time: 24.1 us; the launch traced here: 23.9 us
  Pallas kernels  23.3 us (97%)
  local copies, waits for them, and re-layouts  0.63 us (3%)
    pallas_call x1, Pallas kernels, fused(): pl.pallas_call(kernel, out_shape=pltpu.VMEM((16, 1024), f32), in_specs=[p...  23.3 us
    unnamed x1, local copies, waits for them, and re-layouts  0.63 us

profile of v6, /device:TPU:1, one launch (start us, length us, event | category | flops | bytes accessed | tf_op | source)
XLA Modules:
  0.0 23.9 jit_solution(15666742086747173511)
XLA Ops:
  0.0 23.3 %ladder.1 = f32[16,1024]{1,0:T(8,128)S(1)} custom-call(s32[12]{0:T(128)} %block_hbm.1, s32[12]{0:T(128)} %index_hbm.1, bf16[192,128]{1,0:T(8,128)(2,1)} %bitcast.1, bf16[768,1024]{1,0:T(8,128)(2,1)} %int_hbm.1), custom_call_target="tpu_custom_call" | custom-call | tf_op jit(solution)/shard_map/ladder/pallas_call | solution.py:335
  23.3 0.6 %copy.6 = f32[16,1024]{1,0:T(8,128)} copy(f32[16,1024]{1,0:T(8,128)S(1)} %ladder.1) | data formatting | bytes 131072

commit v7 on v6

--- a/solution.py
+++ b/solution.py
@@ -156,6 +156,7 @@
     sends[...] = jnp.dot(hot, amp, preferred_element_type=jnp.float32).astype(jnp.bfloat16).reshape(16, 32, 128)
     tiles[0, me] = sends[me]
     key_in[me] = key_out[me]
+    out_ref[...] = jnp.zeros_like(out_ref)
 
     pl.semaphore_wait(barrier, n)
 
@@ -180,14 +181,16 @@
     def others(body):
         @loop(n)
         def _(i):
-            to = lax.rem(z + 2 + i // 4, 4) * 4 + lax.rem(me + i, 4)
+            to = lax.rem(2 * (1 - z // 2) + i // 4, 4) * 4 + lax.rem(me + i, 4)
 
             @pl.when(to != me)
             def _():
                 body(to)
 
-    others(lambda to: key_copy(to).start())
-    others(lambda to: tile_copy(to).start())
+    @others
+    def _(to):
+        key_copy(to).start()
+        tile_copy(to).start()
 
     def arrived(s, buffer, sem):
         return pltpu.make_async_remote_copy(
@@ -267,7 +270,6 @@
     def turn(k):
         return lax.rem(k + 2 * (1 - z // 2), 4)
 
-    out_ref[...] = jnp.zeros_like(out_ref)
     load.wait()
     place(0)
 
@@ -279,16 +281,21 @@
     for j in range(4):
         forward(j).wait_recv()
     place(1)
+    multiply(1, 0)
+    core_copy(1, 0).start()
     for k in range(4):
         core_copy(0, k).wait_recv()
 
-    @loop(4)
+    @loop(3)
     def _(k):
         q = turn(k)
         prepare(0, q)
-        multiply(1, k)
-        core_copy(1, k).start()
+        multiply(1, k + 1)
+        core_copy(1, k + 1).start()
         send(0, q)
+
+    prepare(0, turn(3))
+    send(0, turn(3))
 
     for k in range(4):
         core_copy(1, k).wait_recv()
@@ -299,25 +306,7 @@
         prepare(1, q)
         send(1, q)
 
-    @loop(8)
-    def _(i):
-        source = lax.rem(me // 2 + i, 8)
-
-        @pl.when(jnp.logical_or(i > 0, lax.rem(z, 2) != core))
-        def _():
-            arrived(source, landed, sum_rs).wait_recv()
-            out_ref[...] += decode(landed[source])
-
-    @others
-    def _(to):
-        key_copy(to).wait_send()
-        tile_copy(to).wait_send()
-
-    for j in range(4):
-        forward(j).wait_send()
-
-    @loop(2)
-    def _(h):
+    def sent(h):
         for k in range(4):
             core_copy(h, k).wait_send()
 
@@ -326,6 +315,26 @@
             @pl.when(send_to(h, q) != me)
             def _():
                 sum_copy(h, q).wait_send()
+
+    @others
+    def _(to):
+        key_copy(to).wait_send()
+        tile_copy(to).wait_send()
+
+    for j in range(4):
+        forward(j).wait_send()
+    sent(0)
+
+    @loop(8)
+    def _(i):
+        source = lax.rem(me // 2 + i, 8)
+
+        @pl.when(jnp.logical_or(i > 0, lax.rem(z, 2) != core))
+        def _():
+            arrived(source, landed, sum_rs).wait_recv()
+            out_ref[...] += decode(landed[source])
+
+    sent(1)
 
 
 def fused(amplitudes, integrals, tile_block, tile_index):

time: 24.1 us -> 25.2 us (1.046)
  Pallas kernels: 23.3 us -> 24.4 us
    pallas_call x1, Pallas kernels: 23.3 us -> 24.4 us  [fused(): pl.pallas_call(kernel, out_shape=pltpu.VMEM((16, 1024), f32), in_specs=[p...]
where the time goes in v7:
time: 25.2 us; the launch traced here: 25 us
  Pallas kernels  24.4 us (97%)
  local copies, waits for them, and re-layouts  0.63 us (2%)
    pallas_call x1, Pallas kernels, fused(): pl.pallas_call(kernel, out_shape=pltpu.VMEM((16, 1024), f32), in_specs=[p...  24.4 us
    unnamed x1, local copies, waits for them, and re-layouts  0.63 us

profile of v7, /device:TPU:1, one launch (start us, length us, event | category | flops | bytes accessed | tf_op | source)
XLA Modules:
  0.0 25.0 jit_solution(14153126309679695678)
XLA Ops:
  0.0 24.4 %ladder.1 = f32[16,1024]{1,0:T(8,128)S(1)} custom-call(s32[12]{0:T(128)} %block_hbm.1, s32[12]{0:T(128)} %index_hbm.1, bf16[192,128]{1,0:T(8,128)(2,1)} %bitcast.1, bf16[768,1024]{1,0:T(8,128)(2,1)} %int_hbm.1), custom_call_target="tpu_custom_call" | custom-call | tf_op jit(solution)/shard_map/ladder/pallas_call | solution.py:344
  24.4 0.6 %copy.6 = f32[16,1024]{1,0:T(8,128)} copy(f32[16,1024]{1,0:T(8,128)S(1)} %ladder.1) | data formatting | bytes 131072

commit v8 on v7

--- a/solution.py
+++ b/solution.py
@@ -187,10 +187,8 @@
             def _():
                 body(to)
 
-    @others
-    def _(to):
-        key_copy(to).start()
-        tile_copy(to).start()
+    others(lambda to: key_copy(to).start())
+    others(lambda to: tile_copy(to).start())
 
     def arrived(s, buffer, sem):
         return pltpu.make_async_remote_copy(
@@ -281,21 +279,16 @@
     for j in range(4):
         forward(j).wait_recv()
     place(1)
-    multiply(1, 0)
-    core_copy(1, 0).start()
     for k in range(4):
         core_copy(0, k).wait_recv()
 
-    @loop(3)
+    @loop(4)
     def _(k):
         q = turn(k)
         prepare(0, q)
-        multiply(1, k + 1)
-        core_copy(1, k + 1).start()
+        multiply(1, k)
+        core_copy(1, k).start()
         send(0, q)
-
-    prepare(0, turn(3))
-    send(0, turn(3))
 
     for k in range(4):
         core_copy(1, k).wait_recv()

time: 25.2 us -> 23.9 us (0.948)
  Pallas kernels: 24.4 us -> 23.1 us
    pallas_call x1, Pallas kernels: 24.4 us -> 23.1 us  [fused(): pl.pallas_call(kernel, out_shape=pltpu.VMEM((16, 1024), f32), in_specs=[p...]
where the time goes in v8:
time: 23.9 us; the launch traced here: 23.8 us
  Pallas kernels  23.1 us (97%)
  local copies, waits for them, and re-layouts  0.63 us (3%)
    pallas_call x1, Pallas kernels, fused(): pl.pallas_call(kernel, out_shape=pltpu.VMEM((16, 1024), f32), in_specs=[p...  23.1 us
    unnamed x1, local copies, waits for them, and re-layouts  0.63 us

profile of v8, /device:TPU:1, one launch (start us, length us, event | category | flops | bytes accessed | tf_op | source)
XLA Modules:
  0.0 23.8 jit_solution(412718110143328925)
XLA Ops:
  0.0 23.1 %ladder.1 = f32[16,1024]{1,0:T(8,128)S(1)} custom-call(s32[12]{0:T(128)} %block_hbm.1, s32[12]{0:T(128)} %index_hbm.1, bf16[192,128]{1,0:T(8,128)(2,1)} %bitcast.1, bf16[768,1024]{1,0:T(8,128)(2,1)} %int_hbm.1), custom_call_target="tpu_custom_call" | custom-call | tf_op jit(solution)/shard_map/ladder/pallas_call | solution.py:337
  23.1 0.6 %copy.6 = f32[16,1024]{1,0:T(8,128)} copy(f32[16,1024]{1,0:T(8,128)S(1)} %ladder.1) | data formatting | bytes 131072

commit v9 on v8

--- a/solution.py
+++ b/solution.py
@@ -271,10 +271,12 @@
     load.wait()
     place(0)
 
-    @loop(4)
+    @loop(2)
     def _(k):
-        multiply(0, k)
-        core_copy(0, k).start()
+        multiply(0, 2 * k)
+        multiply(0, 2 * k + 1)
+        core_copy(0, 2 * k).start()
+        core_copy(0, 2 * k + 1).start()
 
     for j in range(4):
         forward(j).wait_recv()
@@ -320,7 +322,7 @@
 
     @loop(8)
     def _(i):
-        source = lax.rem(me // 2 + i, 8)
+        source = lax.rem(me // 2 + 8 + i * (1 - 2 * (z // 2)), 8)
 
         @pl.when(jnp.logical_or(i > 0, lax.rem(z, 2) != core))
         def _():

time: 23.9 us -> 23.9 us (level)
  no operation moved by 1% of the time
where the time goes in v9:
time: 23.9 us; the launch traced here: 23.8 us
  Pallas kernels  23.1 us (97%)
  local copies, waits for them, and re-layouts  0.63 us (3%)
    pallas_call x1, Pallas kernels, fused(): pl.pallas_call(kernel, out_shape=pltpu.VMEM((16, 1024), f32), in_specs=[p...  23.1 us
    unnamed x1, local copies, waits for them, and re-layouts  0.63 us

profile of v9, /device:TPU:1, one launch (start us, length us, event | category | flops | bytes accessed | tf_op | source)
XLA Modules:
  0.0 23.8 jit_solution(14360837119573798477)
XLA Ops:
  0.0 23.1 %ladder.1 = f32[16,1024]{1,0:T(8,128)S(1)} custom-call(s32[12]{0:T(128)} %block_hbm.1, s32[12]{0:T(128)} %index_hbm.1, bf16[192,128]{1,0:T(8,128)(2,1)} %bitcast.1, bf16[768,1024]{1,0:T(8,128)(2,1)} %int_hbm.1), custom_call_target="tpu_custom_call" | custom-call | tf_op jit(solution)/shard_map/ladder/pallas_call | solution.py:339
  23.1 0.6 %copy.6 = f32[16,1024]{1,0:T(8,128)} copy(f32[16,1024]{1,0:T(8,128)S(1)} %ladder.1) | data formatting | bytes 131072
